TPU v7x, 32 devices: a whole 2x2x4 slice. The times are simulated.
32 devices in a mesh: grid: 8 (over z, x), cols: 4 (over y, core).
Axes of the slice: x: 2, y: 2, z: 4, core: 2. Of those that a mesh axis runs over, the one named last changes fastest.
Arguments:
- basis: float32 [1024, 3, 16, 1024], P('cols', None, 'grid'), may hold values from -1 to 1
- snapshots: float32 [128, 3, 16, 1024], P('cols', None, 'grid'), may hold values from -60 to 60
- permittivity: float32 [3, 16, 1024], P(None, 'grid'), may hold values from 1 to 10
- labels: int32 [16, 1024], P('grid'), may hold values from 0 to 7
- sigma_table: float32 [8], replicated, may hold values from 0.1 to 10
Outputs:
- new_basis: float32 [128, 3, 16, 1024], P('cols', None, 'grid')
- coefficients: float32 [1024, 128], P('cols')
- cross_terms: float32 [3, 1024, 128], P(None, 'cols')
- block_terms: float32 [3, 128, 128], P(None, 'cols')
All inputs are finite; a program needn't handle non-finite values.
Results may differ from a plain program's by a relative error of at most 0.0003.
Values sent between devices are 32-bit elements; how exact they have to be, the bound alone decides.
A program may use at most 128 MiB of HBM per device.

v0:
```python
import jax
import jax.numpy as jnp
from jax import lax
from jax.sharding import PartitionSpec as P

NY = 32
HIGHEST = lax.Precision.HIGHEST


def padded(shard, sides, width):
    for axis, dim in sides:
        size, length = (lax.axis_size(axis), shard.shape[dim])
        up = [(i, (i + 1) % size) for i in range(size - 1)]
        down = [(j, i) for i, j in up]
        last = lax.slice_in_dim(shard, length - width, length, axis=dim)
        leading = lax.slice_in_dim(shard, 0, width, axis=dim)
        before = lax.ppermute(last, axis, up)
        after = lax.ppermute(leading, axis, down)
        shard = jnp.concatenate([before, shard, after], axis=dim)
    return shard


def cells_dot(left_rows, right_rows):
    left_flat = left_rows.reshape(left_rows.shape[0], -1)
    right_flat = right_rows.reshape(right_rows.shape[0], -1)
    return lax.dot_general(
        left_flat,
        right_flat,
        (((1,), (1,)), ((), ())),
        precision=HIGHEST,
        preferred_element_type=jnp.float32,
    )


def combine_rows(weights, fields):
    flattened = fields.reshape(fields.shape[0], -1)
    output_rows = lax.dot_general(
        weights,
        flattened,
        (((0,), (0,)), ((), ())),
        precision=HIGHEST,
        preferred_element_type=jnp.float32,
    )
    return output_rows.reshape((weights.shape[1],) + fields.shape[1:])


def forward_x(field, row_len):
    padding_cols = jnp.zeros(field.shape[:-1] + (row_len,), field.dtype)
    return jnp.concatenate([field[..., row_len:], padding_cols], axis=-1)


def backward_x(field, row_len):
    padding_cols = jnp.zeros(field.shape[:-1] + (row_len,), field.dtype)
    return jnp.concatenate([padding_cols, field[..., :-row_len]], axis=-1)


def forward_y(field, row_len):
    column_pos = lax.broadcasted_iota(jnp.int32, (field.shape[-1],), 0) % row_len
    padding_cols = jnp.zeros(field.shape[:-1] + (1,), field.dtype)
    shifted = jnp.concatenate([field[..., 1:], padding_cols], axis=-1)
    return jnp.where(column_pos != row_len - 1, shifted, 0.0)


def backward_y(field, row_len):
    column_pos = lax.broadcasted_iota(jnp.int32, (field.shape[-1],), 0) % row_len
    padding_cols = jnp.zeros(field.shape[:-1] + (1,), field.dtype)
    shifted = jnp.concatenate([padding_cols, field[..., :-1]], axis=-1)
    return jnp.where(column_pos != 0, shifted, 0.0)


def curl_curl(extended, row_len):
    field_x = extended[:, 0]
    field_y = extended[:, 1]
    field_z = extended[:, 2]

    def middle(field):
        return field[:, 1:-1]

    def plus_x(field):
        return forward_x(field, row_len) - field

    def minus_x(field):
        return field - backward_x(field, row_len)

    def plus_y(field):
        return forward_y(field, row_len) - field

    def minus_y(field):
        return field - backward_y(field, row_len)

    def second_x(field):
        return forward_x(field, row_len) - 2.0 * field + backward_x(field, row_len)

    def second_y(field):
        return forward_y(field, row_len) - 2.0 * field + backward_y(field, row_len)

    def second_z(field):
        return field[:, 2:] - 2.0 * field[:, 1:-1] + field[:, :-2]

    curl_x = (
        -second_y(middle(field_x))
        - second_z(field_x)
        + minus_y(plus_x(middle(field_y)))
        + plus_x(middle(field_z))
        - plus_x(field_z[:, :-2])
    )
    curl_y = (
        -second_x(middle(field_y))
        - second_z(field_y)
        + minus_x(plus_y(middle(field_x)))
        + plus_y(middle(field_z))
        - plus_y(field_z[:, :-2])
    )
    curl_z = (
        -second_x(middle(field_z))
        - second_y(middle(field_z))
        + minus_x(field_x[:, 2:] - middle(field_x))
        + minus_y(field_y[:, 2:] - middle(field_y))
    )
    return jnp.stack([curl_x, curl_y, curl_z], axis=1)


def lookup_sigma(labels, sigma_table):
    region_ids = jnp.arange(sigma_table.shape[0], dtype=jnp.int32)
    picked = jnp.where(labels[None] == region_ids[:, None, None], sigma_table[:, None, None], 0.0)
    return jnp.sum(picked, axis=0)


def apply_ops(fields, permittivity, conductivity):
    extended = padded(fields, (("grid", 2),), 1)
    curl_term = curl_curl(extended, NY)
    mass_term = permittivity[None] * fields
    loss_term = conductivity[None, None] * fields
    return (curl_term, mass_term, loss_term)


def shards(basis, snapshots, permittivity, labels, sigma_table):
    basis_cols = basis.shape[0]
    snap_cols = snapshots.shape[0]
    total_snap = snap_cols * lax.axis_size("cols")
    unknowns = 3 * snapshots.shape[3] * snapshots.shape[2] * lax.axis_size("grid")
    conductivity = lookup_sigma(labels, sigma_table)
    current = snapshots
    coefficients = jnp.zeros((basis_cols, total_snap), jnp.float32)
    for sweep_index in range(2):
        partial_value = cells_dot(basis, lax.all_gather(current, "cols", axis=0, tiled=True))
        coef_part = lax.psum(partial_value, "grid")
        current = current - lax.psum_scatter(
            combine_rows(coef_part, basis), "cols", scatter_dimension=0, tiled=True
        )
        coefficients = coefficients + coef_part
    finished = lax.all_gather(current, "cols", axis=0, tiled=True)
    own_start = lax.axis_index("cols") * snap_cols
    identity = jnp.eye(total_snap, dtype=jnp.float32)
    gram_sum = lax.psum(cells_dot(finished, finished) / unknowns, "grid")
    lower_factor = jnp.linalg.cholesky(gram_sum)
    inverse = jax.scipy.linalg.solve_triangular(lower_factor, identity, lower=True)
    new_all = combine_rows(inverse.T, finished)
    curl_term, mass_term, loss_term = apply_ops(new_all, permittivity, conductivity)
    own_new = lax.dynamic_slice_in_dim(new_all, own_start, snap_cols, 0)
    cross_part = jnp.stack(
        [cells_dot(basis, curl_term), cells_dot(basis, mass_term), cells_dot(basis, loss_term)],
        axis=0,
    )
    block_part = (
        jnp.stack(
            [
                cells_dot(own_new, curl_term),
                cells_dot(own_new, mass_term),
                cells_dot(own_new, loss_term),
            ],
            axis=0,
        )
        / unknowns
    )
    cross_terms, block_terms = lax.psum((cross_part, block_part), "grid")
    return (own_new, coefficients, cross_terms, block_terms)


def solution(mesh):
    placed = (
        P("cols", None, "grid", None),
        P("cols", None, "grid", None),
        P(None, "grid", None),
        P("grid", None),
        P(),
    )
    return jax.shard_map(
        shards,
        mesh=mesh,
        in_specs=placed,
        out_specs=(
            P("cols", None, "grid", None),
            P("cols", None),
            P(None, "cols", None),
            P(None, "cols", None),
        ),
        check_vma=False,
    )
```

profile of v0, /device:TPU:0, one launch (start us, length us, event | category | flops | bytes accessed | tf_op | source)
XLA Modules:
  0.0 642.6 jit_solution(8649278137576237144)
XLA Ops:
  9.5 31.9 %all-gather.4.cloned.1.call-done = f32[128,3,2,1024]{3,0,2,1:T(8,128)} async-done(((f32[32,3,2,1024]{3,0,2,1:T(8,128)}), f32[128,3,2,1024]{3,0,2,1:T(8,128)}) %all-gather.4.cloned.1.call-update) | async-done | bytes 3145744 | tf_op jit(solution)/shard_map/all_gather | solution.py:146
  41.4 10.8 %fusion.23 = f32[256,128]{1,0:T(8,128)} fusion(f32[128,3,2,1024]{3,0,2,1:T(8,128)} %all-gather.4.cloned.1.call-done, f32[256,3,2,1024]{3,2,1,0:T(2,128)} %param.5), kind=kOutput, calls=%fused_computation.28 | convolution fusion | flops 2415919104 | bytes 9568256 | tf_op jit(solution)/shard_map/dot_general | solution.py:26
  52.2 9.0 %reshape.49 = f32[256,6144]{1,0:T(8,128)} reshape(f32[256,3,2,1024]{3,2,1,0:T(2,128)} %param.5) | data formatting | bytes 12582912 | tf_op jit(solution)/shard_map/reshape | solution.py:24
  61.2 6.6 %copy.42 = f32[6144,256]{1,0:T(8,128)} copy(f32[6144,256]{0,1:T(8,128)} %bitcast.112) | data formatting | bytes 12582912 | tf_op jit(solution)/shard_map/dot_general | solution.py:37
  67.8 54.2 %all-reduce.19.cloned.1.call-done = f32[256,128]{1,0:T(8,128)} async-done(((f32[256,128]{1,0:T(8,128)}), f32[256,128]{1,0:T(8,128)}) %all-reduce.19.cloned.1.call-update) | async-done | bytes 131088 | tf_op jit(solution)/shard_map/psum | solution.py:147
  122.0 11.2 %fusion.63 = f32[128,3,2,1024]{3,0,2,1:T(8,128)} fusion(f32[3,2,1024,256]{3,2,1,0:T(8,128)} %bitcast.110, f32[256,128]{1,0:T(8,128)} %all-reduce.19.cloned.1.call-done), kind=kOutput, calls=%fused_computation.61 | convolution fusion | flops 2415919104 | bytes 9568256 | tf_op jit(solution)/shard_map/dot_general | solution.py:37
  133.6 37.1 %reduce-scatter.3.cloned.1.call-done = f32[32,3,2,1024]{3,0,2,1:T(8,128)} async-done(((f32[128,3,2,1024]{3,0,2,1:T(8,128)}), f32[32,3,2,1024]{3,0,2,1:T(8,128)}) %reduce-scatter.3.cloned.1.call-update) | async-done | bytes 786448 | tf_op jit(solution)/shard_map/reduce_scatter | solution.py:148
  173.1 28.6 %all-gather.6.cloned.1.call-done = f32[128,3,2,1024]{3,0,2,1:T(8,128)} async-done(((f32[32,3,2,1024]{3,0,2,1:T(8,128)}), f32[128,3,2,1024]{3,0,2,1:T(8,128)}) %all-gather.6.cloned.1.call-update) | async-done | bytes 3145744 | tf_op jit(solution)/shard_map/all_gather | solution.py:146
  201.7 10.7 %fusion.26 = f32[256,128]{1,0:T(8,128)} fusion(f32[128,3,2,1024]{3,0,2,1:T(8,128)} %all-gather.6.cloned.1.call-done, f32[256,3,2,1024]{3,2,1,0:T(2,128)} %param.5), kind=kOutput, calls=%fused_computation.29 | convolution fusion | flops 2415919104 | bytes 9568256 | tf_op jit(solution)/shard_map/dot_general | solution.py:26
  212.4 69.8 %all-reduce.21.cloned.1.call-done = f32[256,128]{1,0:T(8,128)} async-done(((f32[256,128]{1,0:T(8,128)}), f32[256,128]{1,0:T(8,128)}) %all-reduce.21.cloned.1.call-update) | async-done | bytes 131088 | tf_op jit(solution)/shard_map/psum | solution.py:147
  282.2 11.2 %fusion.61 = f32[128,3,2,1024]{3,0,2,1:T(8,128)} fusion(f32[3,2,1024,256]{3,2,1,0:T(8,128)} %bitcast.111, f32[256,128]{1,0:T(8,128)} %all-reduce.21.cloned.1.call-done), kind=kOutput, calls=%fused_computation.59 | convolution fusion | flops 2415919104 | bytes 9568256 | tf_op jit(solution)/shard_map/dot_general | solution.py:37
  293.5 37.3 %reduce-scatter.5.cloned.1.call-done = f32[32,3,2,1024]{3,0,2,1:T(8,128)} async-done(((f32[128,3,2,1024]{3,0,2,1:T(8,128)}), f32[32,3,2,1024]{3,0,2,1:T(8,128)}) %reduce-scatter.5.cloned.1.call-update) | async-done | bytes 786448 | tf_op jit(solution)/shard_map/reduce_scatter | solution.py:148
  333.4 28.2 %all-gather.8.cloned.1.call-done = f32[128,3,2,1024]{3,0,2,1:T(8,128)} async-done(((f32[32,3,2,1024]{3,0,2,1:T(8,128)}), f32[128,3,2,1024]{3,0,2,1:T(8,128)}) %all-gather.8.cloned.1.call-update) | async-done | bytes 3145744 | tf_op jit(solution)/shard_map/all_gather | solution.py:152
  361.7 6.3 fusion.42
  370.4 66.2 %all-reduce.23.cloned.1.call-done = f32[128,128]{0,1:T(8,128)} async-done(((f32[128,128]{0,1:T(8,128)}), f32[128,128]{0,1:T(8,128)}) %all-reduce.23.cloned.1.call-update) | async-done | bytes 65552 | tf_op jit(solution)/shard_map/psum | solution.py:155
  438.4 11.7 %cholesky.17 = f32[128,128]{1,0:T(8,128)S(1)} custom-call(f32[128,128]{1,0:T(8,128)S(1)} %fusion.67), custom_call_target="Cholesky" | custom-call | tf_op jit(solution)/shard_map/jit(cholesky)/cholesky | solution.py:156
  451.4 9.8 %custom-call.7 = f32[1,128,128]{1,2,0:T(8,128)S(1)} custom-call(f32[1,128,128]{2,1,0:T(8,128)S(1)} %fusion.65), custom_call_target="InvertDiagBlocksLowerTriangular" | custom-call | tf_op jit(solution)/shard_map/jit(_solve_triangular)/triangular_solve | solution.py:157
  461.5 4.7 fusion.10
  479.0 9.9 %fusion.37 = f32[1,256,128]{1,2,0:T(8,128)S(1)} fusion(f32[256,3,2,1024]{3,2,1,0:T(2,128)} %param.5, f32[128,3,2,1024]{3,0,2,1:T(8,128)S(1)} %fusion.10, f32[2,1024]{1,0:T(2,128)S(1)} %select_reduce_fusion), kind=kOutput, calls=%fused_computation.32 | convolution fusion | flops 2416705536 | bytes 9576448 | tf_op jit(solution)/shard_map/dot_general | solution.py:26
  488.9 7.2 %fusion.32 = f32[1,256,128]{1,2,0:T(8,128)S(1)} fusion(f32[256,3,2,1024]{3,2,1,0:T(2,128)S(1)} %bitcast.109, f32[128,3,2,1024]{3,0,2,1:T(8,128)S(1)} %fusion.10, f32[3,2,1024]{2,1,0:T(2,128)S(1)} %copy-done.15), kind=kOutput, calls=%fused_computation.31 | convolution fusion | flops 2416705536 | bytes 9592832 | tf_op jit(solution)/shard_map/dot_general | solution.py:26
  496.2 41.0 %collective-permute-done = f32[128,3,1,1024]{3,0,2,1:T(8,128)} collective-permute-done((f32[128,3,1,1024]{3,0,2,1:T(8,128)}, f32[128,3,1,1024]{3,0,2,1:T(8,128)}, u32[]{:S(2)}, u32[]{:S(2)}) %collective-permute-start) | collective-permute-done | bytes 1572896 | tf_op jit(solution)/shard_map/ppermute | solution.py:17
  553.0 7.3 %fusion.29 = f32[1,256,128]{1,2,0:T(8,128)S(1)} fusion(f32[256,3,2,1024]{3,2,1,0:T(2,128)S(1)} %bitcast.109, f32[128,1,2,1024]{3,0,2,1:T(8,128)S(1)} %add_bitcast_fusion, f32[128,1,2,1024]{3,0,2,1:T(8,128)S(1)} %fusion.54, f32[128,1,2,1024]{3,0,2,1:T(8,128)S(1)} %get-tuple-element.19), kind=kOutput, calls=%fused_computation.30 | convolution fusion | flops 2417491968 | bytes 9568256 | tf_op jit(solution)/shard_map/dot_general | solution.py:26
  570.3 37.2 %psum.39 = f32[3,32,128]{2,1,0:T(8,128)} all-reduce(f32[3,32,128]{2,1,0:T(8,128)S(1)} %maximum_multiply_fusion), channel_id=1, replica_groups=mesh['grid'=8,'cols'=4] {'grid'}, use_global_device_ids=true, to_apply=%region_9.10 | all-reduce | flops 12288 | bytes 98304 | tf_op jit(solution)/shard_map/psum | solution.py:176
  607.5 26.2 %all-reduce.25.cloned.1.call-done = f32[3,256,128]{1,2,0:T(8,128)} async-done(((f32[3,256,128]{1,2,0:T(8,128)}), f32[3,256,128]{1,2,0:T(8,128)}) %all-reduce.25.cloned.1.call-update) | async-done | bytes 393232 | tf_op jit(solution)/shard_map/psum | solution.py:176
  (92 shorter events, 53.7 us)
Async XLA Ops:
  7.2 34.2 %all-gather.4.cloned.1.call-start = ((), (), s32[]{:S(2)}) async-start(), calls=%async_computation.2 | async-start | bytes 3932160 | tf_op jit(solution)/shard_map/all_gather | solution.py:146
  9.5 112.6 %all-reduce.19.cloned.1.call-start = ((), (), s32[]{:S(2)}) async-start(), calls=%async_computation.3 | async-start | bytes 262144 | tf_op jit(solution)/shard_map/psum | solution.py:147
  52.2 118.5 %reduce-scatter.3.cloned.1.call-start = ((), (), s32[]{:S(2)}) async-start(), calls=%async_computation.4 | async-start | bytes 3932160 | tf_op jit(solution)/shard_map/reduce_scatter | solution.py:148
  133.3 37.4 %copy-start.12 = (f32[32,3,2,1024]{3,2,1,0:T(2,128)S(1)}, f32[32,3,2,1024]{3,2,1,0:T(2,128)}, u32[]{:S(2)}) copy-start(f32[32,3,2,1024]{3,2,1,0:T(2,128)} %param.6) | copy-start | bytes 2359300
  133.3 68.4 %all-gather.6.cloned.1.call-start = ((), (), s32[]{:S(2)}) async-start(), calls=%async_computation.5 | async-start | bytes 3932160 | tf_op jit(solution)/shard_map/all_gather | solution.py:146
  173.0 109.2 %all-reduce.21.cloned.1.call-start = ((), (), s32[]{:S(2)}) async-start(), calls=%async_computation.6 | async-start | bytes 262144 | tf_op jit(solution)/shard_map/psum | solution.py:147
  212.4 118.5 %reduce-scatter.5.cloned.1.call-start = ((), (), s32[]{:S(2)}) async-start(), calls=%async_computation.7 | async-start | bytes 3932160 | tf_op jit(solution)/shard_map/reduce_scatter | solution.py:148
  293.5 37.4 %copy-start.3 = (f32[32,3,2,1024]{3,0,2,1:T(8,128)S(1)}, f32[32,3,2,1024]{3,0,2,1:T(8,128)}, u32[]{:S(2)}) copy-start(f32[32,3,2,1024]{3,0,2,1:T(8,128)} %copy_subtract_fusion) | copy-start | bytes 2359300
  293.5 68.2 %all-gather.8.cloned.1.call-start = ((), (), s32[]{:S(2)}) async-start(), calls=%async_computation.8 | async-start | bytes 3932160 | tf_op jit(solution)/shard_map/all_gather | solution.py:152
  333.0 103.6 %all-reduce.23.cloned.1.call-start = ((), (), s32[]{:S(2)}) async-start(), calls=%async_computation.9 | async-start | bytes 131072 | tf_op jit(solution)/shard_map/psum | solution.py:155
  361.7 6.4 copy-start
  368.0 265.7 %all-reduce.25.cloned.1.call-start = ((), (), s32[]{:S(2)}) async-start(), calls=%async_computation.10 | async-start | bytes 786432 | tf_op jit(solution)/shard_map/psum | solution.py:176
  466.2 7.9 %copy-start.16 = (s32[2,1024]{1,0:T(2,128)S(1)}, s32[2,1024]{1,0:T(2,128)}, u32[]{:S(2)}) copy-start(s32[2,1024]{1,0:T(2,128)} %param.8) | copy-start | bytes 24580
  466.2 7.9 %copy-start.17 = (f32[8]{0:T(128)S(1)}, f32[8]{0:T(128)}, u32[]{:S(2)}) copy-start(f32[8]{0:T(128)} %param.9) | copy-start | bytes 100
  466.2 8.0 %copy-start.13 = (f32[256,128]{1,0:T(8,128)S(1)}, f32[256,128]{1,0:T(8,128)}, u32[]{:S(2)}) copy-start(f32[256,128]{1,0:T(8,128)} %all-reduce.19.cloned.1.call-done) | copy-start | bytes 393220
  466.2 8.0 %copy-start.14 = (f32[256,128]{1,0:T(8,128)S(1)}, f32[256,128]{1,0:T(8,128)}, u32[]{:S(2)}) copy-start(f32[256,128]{1,0:T(8,128)} %all-reduce.21.cloned.1.call-done) | copy-start | bytes 393220
  466.2 9.6 %copy-start.15 = (f32[3,2,1024]{2,1,0:T(2,128)S(1)}, f32[3,2,1024]{2,1,0:T(2,128)}, u32[]{:S(2)}) copy-start(f32[3,2,1024]{2,1,0:T(2,128)} %param.7) | copy-start | bytes 73732
  468.1 69.1 %collective-permute-start = (f32[128,3,1,1024]{3,0,2,1:T(8,128)}, f32[128,3,1,1024]{3,0,2,1:T(8,128)}, u32[]{:S(2)}, u32[]{:S(2)}) collective-permute-start(f32[128,3,1,1024]{3,0,2,1:T(8,128)} %get-tuple-element.21), channel_id=1, source_target_pairs={{0,4},{4,8},{8,12},{12,16},{16,20},{20,24},{24,28},{1,5},{5,9},{9,... | collective-permute-start | bytes 4718600 | tf_op jit(solution)/shard_map/ppermute | solution.py:17
  472.6 64.6 %collective-permute-start.1 = (f32[128,3,1,1024]{3,0,2,1:T(8,128)}, f32[128,3,1,1024]{3,0,2,1:T(8,128)}, u32[]{:S(2)}, u32[]{:S(2)}) collective-permute-start(f32[128,3,1,1024]{3,0,2,1:T(8,128)} %get-tuple-element.22), channel_id=1, source_target_pairs={{4,0},{8,4},{12,8},{16,12},{20,16},{24,20},{28,24},{5,1},{9,5},{13... | collective-permute-start | bytes 4718600 | tf_op jit(solution)/shard_map/ppermute | solution.py:18
  475.8 13.0 %slice-start = ((s8[6291456]{0:T(1024)(128)(4,1)}), s8[4194304]{0:T(1024)(128)(4,1)S(1)}, s32[]{:S(2)}) async-start(s8[6291456]{0:T(1024)(128)(4,1)} %bitcast.108), calls=%async_computation.11 | async-start | bytes 8388608
  479.0 9.9 %slice-start.1 = ((s8[6291456]{0:T(1024)(128)(4,1)}), s8[2097152]{0:T(1024)(128)(4,1)S(1)}, s32[]{:S(2)}) async-start(s8[6291456]{0:T(1024)(128)(4,1)} %bitcast.108), calls=%async_computation.12 | async-start | bytes 4194304
  553.0 7.3 %copy-start.9 = (f32[128,1,2,1024]{3,0,2,1:T(8,128)}, f32[128,1,2,1024]{3,0,2,1:T(8,128)S(1)}, u32[]{:S(2)}) copy-start(f32[128,1,2,1024]{3,0,2,1:T(8,128)S(1)} %add_bitcast_fusion) | copy-start | bytes 3145732
  561.1 6.0 copy-start.5
  561.1 6.0 copy-start.7
  (7 other events, 19.8 us)
Sparse Core Ops, SparseCore 0:
  10.1 31.2 all-gather.3
  52.3 69.6 all-reduce.18
  133.4 37.2 reduce-scatter.2
  173.1 28.5 all-gather.5
  212.5 69.6 all-reduce.20
  293.6 37.2 reduce-scatter.4
  333.1 28.5 all-gather.7
  368.1 68.4 all-reduce.22
  561.2 72.4 all-reduce.24
where the time goes:
time: 652 us; the launch traced here: 643 us
  waiting for transfers between devices  421 us (65%)
  matrix products  90.2 us (14%)
  other arithmetic  38.7 us (6%)
  blocking collectives  37.2 us (6%)
  local copies, waits for them, and re-layouts  34 us (5%)
  between operations  14.7 us (2%)
  starting transfers between devices  6.98 us (1%)
    psum x2, waiting for transfers between devices, shards(): coef_part = lax.psum(partial_value, 'grid')  124 us
    reduce_scatter x2, waiting for transfers between devices, shards(): lax.psum_scatter(combine_rows(coef_part, basis), 'cols', scatter_dimensio...  74.4 us
    psum x1, waiting for transfers between devices, shards(): gram_sum = lax.psum(cells_dot(finished, finished) / unknowns, 'grid')  66.2 us
    dot_general x9, matrix products, cells_dot(): lax.dot_general(left_flat, right_flat, (((1,), (1,)), ((), ())), precisio...  62.8 us
    all_gather x2, waiting for transfers between devices, shards(): lax.all_gather(current, 'cols', axis=0, tiled=True)  60.5 us
    ppermute x1, waiting for transfers between devices, padded(): before = lax.ppermute(last, axis, up)  41 us
    psum x1, blocking collectives, shards(): cross_terms, block_terms = lax.psum((cross_part, block_part), 'grid')  37.2 us
    all_gather x1, waiting for transfers between devices, shards(): finished = lax.all_gather(current, 'cols', axis=0, tiled=True)  28.2 us
  transfers between devices with their start and end apart: 11, of which 10 were waited for; matrix products, arithmetic and copies ran while one was open for 7% of the time, Pallas kernels for 0%

commit v1 on v0

--- a/solution.py
+++ b/solution.py
@@ -149,7 +149,25 @@
             combine_rows(coef_part, basis), "cols", scatter_dimension=0, tiled=True
         )
         coefficients = coefficients + coef_part
-    finished = lax.all_gather(current, "cols", axis=0, tiled=True)
+    count, index, width_2 = (lax.axis_size("cols"), lax.axis_index("cols"), current.shape[0])
+    upward = [(i_2, (i_2 + 1) % count) for i_2 in range(count)]
+    behind = [(i_2, (i_2 - 1) % count) for i_2 in range(count)]
+    finished = jnp.zeros(
+        (*current.shape[:0], count * width_2, *current.shape[0 + 1 :]), current.dtype
+    )
+    finished = lax.dynamic_update_slice_in_dim(finished, current, index * width_2, axis=0)
+    from_left = from_right = current
+    half = count // 2
+    for step in range(1, half + 1):
+        from_left = lax.ppermute(from_left, "cols", upward)
+        finished = lax.dynamic_update_slice_in_dim(
+            finished, from_left, (index - step) % count * width_2, axis=0
+        )
+        if step < count - half:
+            from_right = lax.ppermute(from_right, "cols", behind)
+            finished = lax.dynamic_update_slice_in_dim(
+                finished, from_right, (index + step) % count * width_2, axis=0
+            )
     own_start = lax.axis_index("cols") * snap_cols
     identity = jnp.eye(total_snap, dtype=jnp.float32)
     gram_sum = lax.psum(cells_dot(finished, finished) / unknowns, "grid")

time: 652 us -> 753 us (1.15)
  local copies, waits for them, and re-layouts: 34 us -> 142 us
    dynamic_update_slice x0 -> x4, local copies, waits for them, and re-layouts: none -> 99.9 us  [the longest x2 51.2 us: shards(): lax.dynamic_update_slice_in_dim(finished, from_left, (index - step) % cou...]
    all_gather x1 -> x0, waiting for transfers between devices: 28.2 us -> none  [shards(): finished = lax.all_gather(current, 'cols', axis=0, tiled=True)]
    ppermute x0 -> x3, waiting for transfers between devices: none -> 17.9 us  [the longest x2 17.8 us: shards(): from_left = lax.ppermute(from_left, 'cols', upward)]
    ppermute x0 -> x3, local copies, waits for them, and re-layouts: none -> 9.36 us  [the longest x2 6.24 us: shards(): from_left = lax.ppermute(from_left, 'cols', upward)]
  transfers between devices with their start and end apart: 11 -> 13, of which waited for: 10 -> 10; matrix products, arithmetic and copies ran while one was open for 7% -> 17% of each run, Pallas kernels for 0% -> 0%
where the time goes in v1:
time: 753 us; the launch traced here: 743 us
  waiting for transfers between devices  417 us (55%)
  local copies, waits for them, and re-layouts  142 us (19%)
  matrix products  86.9 us (12%)
  blocking collectives  37.2 us (5%)
  other arithmetic  36.7 us (5%)
  between operations  14.9 us (2%)
  starting transfers between devices  8.18 us (1%)
    psum x2, waiting for transfers between devices, shards(): coef_part = lax.psum(partial_value, 'grid')  124 us
    reduce_scatter x2, waiting for transfers between devices, shards(): lax.psum_scatter(combine_rows(coef_part, basis), 'cols', scatter_dimensio...  74.2 us
    psum x1, waiting for transfers between devices, shards(): gram_sum = lax.psum(cells_dot(finished, finished) / unknowns, 'grid')  69.2 us
    all_gather x2, waiting for transfers between devices, shards(): lax.all_gather(current, 'cols', axis=0, tiled=True)  60.5 us
    dot_general x9, matrix products, cells_dot(): lax.dot_general(left_flat, right_flat, (((1,), (1,)), ((), ())), precisio...  59.4 us
    dynamic_update_slice x2, local copies, waits for them, and re-layouts, shards(): lax.dynamic_update_slice_in_dim(finished, from_left, (index - step) % cou...  51.2 us
    ppermute x1, waiting for transfers between devices, padded(): before = lax.ppermute(last, axis, up)  45.3 us
    psum x1, blocking collectives, shards(): cross_terms, block_terms = lax.psum((cross_part, block_part), 'grid')  37.2 us
  transfers between devices with their start and end apart: 13, of which 10 were waited for; matrix products, arithmetic and copies ran while one was open for 17% of the time, Pallas kernels for 0%

profile of v1, /device:TPU:0, one launch (start us, length us, event | category | flops | bytes accessed | tf_op | source)
XLA Modules:
  0.0 743.1 jit_solution(14907837654088508062)
XLA Ops:
  9.5 31.9 %all-gather.3.cloned.1.call-done = f32[128,3,2,1024]{3,0,2,1:T(8,128)} async-done(((f32[32,3,2,1024]{3,0,2,1:T(8,128)}), f32[128,3,2,1024]{3,0,2,1:T(8,128)}) %all-gather.3.cloned.1.call-update) | async-done | bytes 3145744 | tf_op jit(solution)/shard_map/all_gather | solution.py:146
  41.4 10.8 %fusion.23 = f32[256,128]{1,0:T(8,128)} fusion(f32[128,3,2,1024]{3,0,2,1:T(8,128)} %all-gather.3.cloned.1.call-done, f32[256,3,2,1024]{3,2,1,0:T(2,128)} %param.5), kind=kOutput, calls=%fused_computation.28 | convolution fusion | flops 2415919104 | bytes 9568256 | tf_op jit(solution)/shard_map/dot_general | solution.py:26
  52.2 9.0 %reshape.49 = f32[256,6144]{1,0:T(8,128)} reshape(f32[256,3,2,1024]{3,2,1,0:T(2,128)} %param.5) | data formatting | bytes 12582912 | tf_op jit(solution)/shard_map/reshape | solution.py:24
  67.8 54.2 %all-reduce.19.cloned.1.call-done = f32[256,128]{1,0:T(8,128)} async-done(((f32[256,128]{1,0:T(8,128)}), f32[256,128]{1,0:T(8,128)}) %all-reduce.19.cloned.1.call-update) | async-done | bytes 131088 | tf_op jit(solution)/shard_map/psum | solution.py:147
  122.0 11.2 %fusion.63 = f32[128,3,2,1024]{3,0,2,1:T(8,128)} fusion(f32[3,2,1024,256]{3,2,1,0:T(8,128)} %bitcast.110, f32[256,128]{1,0:T(8,128)} %all-reduce.19.cloned.1.call-done), kind=kOutput, calls=%fused_computation.61 | convolution fusion | flops 2415919104 | bytes 9568256 | tf_op jit(solution)/shard_map/dot_general | solution.py:37
  133.8 36.9 %reduce-scatter.3.cloned.1.call-done = f32[32,3,2,1024]{3,0,2,1:T(8,128)} async-done(((f32[128,3,2,1024]{3,0,2,1:T(8,128)}), f32[32,3,2,1024]{3,0,2,1:T(8,128)}) %reduce-scatter.3.cloned.1.call-update) | async-done | bytes 786448 | tf_op jit(solution)/shard_map/reduce_scatter | solution.py:148
  173.1 28.6 %all-gather.5.cloned.1.call-done = f32[128,3,2,1024]{3,0,2,1:T(8,128)} async-done(((f32[32,3,2,1024]{3,0,2,1:T(8,128)}), f32[128,3,2,1024]{3,0,2,1:T(8,128)}) %all-gather.5.cloned.1.call-update) | async-done | bytes 3145744 | tf_op jit(solution)/shard_map/all_gather | solution.py:146
  201.7 10.7 %fusion.26 = f32[256,128]{1,0:T(8,128)} fusion(f32[128,3,2,1024]{3,0,2,1:T(8,128)} %all-gather.5.cloned.1.call-done, f32[256,3,2,1024]{3,2,1,0:T(2,128)} %param.5), kind=kOutput, calls=%fused_computation.29 | convolution fusion | flops 2415919104 | bytes 9568256 | tf_op jit(solution)/shard_map/dot_general | solution.py:26
  212.4 69.8 %all-reduce.21.cloned.1.call-done = f32[256,128]{1,0:T(8,128)} async-done(((f32[256,128]{1,0:T(8,128)}), f32[256,128]{1,0:T(8,128)}) %all-reduce.21.cloned.1.call-update) | async-done | bytes 131088 | tf_op jit(solution)/shard_map/psum | solution.py:147
  282.2 11.2 %fusion.61 = f32[128,3,2,1024]{3,0,2,1:T(8,128)} fusion(f32[3,2,1024,256]{3,2,1,0:T(8,128)} %bitcast.111, f32[256,128]{1,0:T(8,128)} %all-reduce.21.cloned.1.call-done), kind=kOutput, calls=%fused_computation.59 | convolution fusion | flops 2415919104 | bytes 9568256 | tf_op jit(solution)/shard_map/dot_general | solution.py:37
  293.5 37.3 %reduce-scatter.5.cloned.1.call-done = f32[32,3,2,1024]{3,0,2,1:T(8,128)} async-done(((f32[128,3,2,1024]{3,0,2,1:T(8,128)}), f32[32,3,2,1024]{3,0,2,1:T(8,128)}) %reduce-scatter.5.cloned.1.call-update) | async-done | bytes 786448 | tf_op jit(solution)/shard_map/reduce_scatter | solution.py:148
  334.7 17.8 %collective-permute-done = f32[32,3,2,1024]{3,0,2,1:T(8,128)} collective-permute-done((f32[32,3,2,1024]{3,0,2,1:T(8,128)}, f32[32,3,2,1024]{3,0,2,1:T(8,128)}, u32[]{:S(2)}, u32[]{:S(2)}) %collective-permute-start) | collective-permute-done | bytes 786464 | tf_op jit(solution)/shard_map/ppermute | solution.py:162
  356.1 23.0 %dynamic_update_slice.12 = f32[128,3,2,1024]{0,3,2,1:T(8,128)S(1)} dynamic-update-slice(f32[128,3,2,1024]{0,3,2,1:T(8,128)S(1)} %broadcast_in_dim.58, f32[32,3,2,1024]{0,3,2,1:T(8,128)} %copy.53, s32[]{:T(128)S(6)} %select_n.94, s32[]{:T(128)} %constant.117.clone.1, s32[]{:T(128)} %constant.117.clone.1, s32[]{:T(128)} %constant.117.clone.1) | dynamic-update-slice | bytes 1572868 | tf_op jit(solution)/shard_map/dynamic_update_slice | solution.py:158
  382.3 25.6 %dynamic_update_slice.13 = f32[128,3,2,1024]{0,3,2,1:T(8,128)S(1)} dynamic-update-slice(f32[128,3,2,1024]{0,3,2,1:T(8,128)S(1)} %dynamic_update_slice.12, f32[32,3,2,1024]{0,3,2,1:T(8,128)} %copy.54, s32[]{:T(128)S(6)} %select_n.96, s32[]{:T(128)} %constant.117.clone.1, s32[]{:T(128)} %constant.117.clone.1, s32[]{:T(128)} %constant.117.clone.1) | dynamic-update-slice | bytes 1572868 | tf_op jit(solution)/shard_map/dynamic_update_slice | solution.py:163
  411.1 25.6 %dynamic_update_slice.14 = f32[128,3,2,1024]{0,3,2,1:T(8,128)S(1)} dynamic-update-slice(f32[128,3,2,1024]{0,3,2,1:T(8,128)S(1)} %dynamic_update_slice.13, f32[32,3,2,1024]{0,3,2,1:T(8,128)} %copy.55, s32[]{:T(128)S(6)} %select_n.98, s32[]{:T(128)} %constant.117.clone.1, s32[]{:T(128)} %constant.117.clone.1, s32[]{:T(128)} %constant.117.clone.1) | dynamic-update-slice | bytes 1572868 | tf_op jit(solution)/shard_map/dynamic_update_slice | solution.py:168
  439.8 25.6 %dynamic_update_slice.15 = f32[128,3,2,1024]{0,3,2,1:T(8,128)S(1)} dynamic-update-slice(f32[128,3,2,1024]{0,3,2,1:T(8,128)S(1)} %dynamic_update_slice.14, f32[32,3,2,1024]{0,3,2,1:T(8,128)} %copy.56, s32[]{:T(128)S(6)} %select_n.100, s32[]{:T(128)} %constant.117.clone.1, s32[]{:T(128)} %constant.117.clone.1, s32[]{:T(128)} %constant.117.clone.1) | dynamic-update-slice | bytes 1572868 | tf_op jit(solution)/shard_map/dynamic_update_slice | solution.py:163
  471.5 69.2 %all-reduce.23.cloned.1.call-done = f32[128,128]{0,1:T(8,128)} async-done(((f32[128,128]{0,1:T(8,128)}), f32[128,128]{0,1:T(8,128)}) %all-reduce.23.cloned.1.call-update) | async-done | bytes 65552 | tf_op jit(solution)/shard_map/psum | solution.py:173
  542.5 11.7 %cholesky.17 = f32[128,128]{1,0:T(8,128)S(1)} custom-call(f32[128,128]{1,0:T(8,128)S(1)} %fusion.67), custom_call_target="Cholesky" | custom-call | tf_op jit(solution)/shard_map/jit(cholesky)/cholesky | solution.py:174
  555.5 9.8 %custom-call.7 = f32[1,128,128]{1,2,0:T(8,128)S(1)} custom-call(f32[1,128,128]{2,1,0:T(8,128)S(1)} %fusion.65), custom_call_target="InvertDiagBlocksLowerTriangular" | custom-call | tf_op jit(solution)/shard_map/jit(_solve_triangular)/triangular_solve | solution.py:175
  587.2 7.2 fusion.32
  594.4 45.3 %collective-permute-done.3 = f32[128,3,1,1024]{3,0,2,1:T(8,128)S(1)} collective-permute-done((f32[128,3,1,1024]{3,0,2,1:T(8,128)S(1)}, f32[128,3,1,1024]{3,0,2,1:T(8,128)S(1)}, u32[]{:S(2)}, u32[]{:S(2)}) %collective-permute-start.3) | collective-permute-done | bytes 1572896 | tf_op jit(solution)/shard_map/ppermute | solution.py:17
  653.4 7.2 fusion.29
  670.7 37.2 %psum.39 = f32[3,32,128]{2,1,0:T(8,128)} all-reduce(f32[3,32,128]{2,1,0:T(8,128)S(1)} %maximum_multiply_fusion), channel_id=1, replica_groups=mesh['grid'=8,'cols'=4] {'grid'}, use_global_device_ids=true, to_apply=%region_9.10 | all-reduce | flops 12288 | bytes 98304 | tf_op jit(solution)/shard_map/psum | solution.py:194
  707.9 26.2 %all-reduce.25.cloned.1.call-done = f32[3,256,128]{1,2,0:T(8,128)} async-done(((f32[3,256,128]{1,2,0:T(8,128)}), f32[3,256,128]{1,2,0:T(8,128)}) %all-reduce.25.cloned.1.call-update) | async-done | bytes 393232 | tf_op jit(solution)/shard_map/psum | solution.py:194
  (103 shorter events, 84.9 us)
Async XLA Ops:
  7.2 34.2 %all-gather.3.cloned.1.call-start = ((), (), s32[]{:S(2)}) async-start(), calls=%async_computation.2 | async-start | bytes 3932160 | tf_op jit(solution)/shard_map/all_gather | solution.py:146
  9.5 112.6 %all-reduce.19.cloned.1.call-start = ((), (), s32[]{:S(2)}) async-start(), calls=%async_computation.3 | async-start | bytes 262144 | tf_op jit(solution)/shard_map/psum | solution.py:147
  52.2 118.5 %reduce-scatter.3.cloned.1.call-start = ((), (), s32[]{:S(2)}) async-start(), calls=%async_computation.4 | async-start | bytes 3932160 | tf_op jit(solution)/shard_map/reduce_scatter | solution.py:148
  133.3 37.4 %copy-start.12 = (f32[32,3,2,1024]{3,2,1,0:T(2,128)S(1)}, f32[32,3,2,1024]{3,2,1,0:T(2,128)}, u32[]{:S(2)}) copy-start(f32[32,3,2,1024]{3,2,1,0:T(2,128)} %param.6) | copy-start | bytes 2359300
  133.3 68.4 %all-gather.5.cloned.1.call-start = ((), (), s32[]{:S(2)}) async-start(), calls=%async_computation.5 | async-start | bytes 3932160 | tf_op jit(solution)/shard_map/all_gather | solution.py:146
  173.0 109.2 %all-reduce.21.cloned.1.call-start = ((), (), s32[]{:S(2)}) async-start(), calls=%async_computation.6 | async-start | bytes 262144 | tf_op jit(solution)/shard_map/psum | solution.py:147
  212.4 118.5 %reduce-scatter.5.cloned.1.call-start = ((), (), s32[]{:S(2)}) async-start(), calls=%async_computation.7 | async-start | bytes 3932160 | tf_op jit(solution)/shard_map/reduce_scatter | solution.py:148
  293.5 37.4 %copy-start.3 = (f32[32,3,2,1024]{3,0,2,1:T(8,128)S(1)}, f32[32,3,2,1024]{3,0,2,1:T(8,128)}, u32[]{:S(2)}) copy-start(f32[32,3,2,1024]{3,0,2,1:T(8,128)} %copy_subtract_fusion) | copy-start | bytes 2359300
  293.5 247.2 %all-reduce.23.cloned.1.call-start = ((), (), s32[]{:S(2)}) async-start(), calls=%async_computation.8 | async-start | bytes 131072 | tf_op jit(solution)/shard_map/psum | solution.py:173
  333.0 19.6 %collective-permute-start = (f32[32,3,2,1024]{3,0,2,1:T(8,128)}, f32[32,3,2,1024]{3,0,2,1:T(8,128)}, u32[]{:S(2)}, u32[]{:S(2)}) collective-permute-start(f32[32,3,2,1024]{3,0,2,1:T(8,128)} %sub.82), channel_id=1, source_target_pairs={{0,1},{1,2},{2,3},{3,0},{4,5},{5,6},{6,7},{7,4},{8,9},{9,10},{10,1... | collective-permute-start | bytes 2359304 | tf_op jit(solution)/shard_map/ppermute | solution.py:162
  333.0 75.0 %collective-permute-start.1 = (f32[32,3,2,1024]{3,0,2,1:T(8,128)}, f32[32,3,2,1024]{3,0,2,1:T(8,128)}, u32[]{:S(2)}, u32[]{:S(2)}) collective-permute-start(f32[32,3,2,1024]{3,0,2,1:T(8,128)} %sub.82), channel_id=1, source_target_pairs={{0,3},{1,0},{2,1},{3,2},{4,7},{5,4},{6,5},{7,6},{8,11},{9,8},{10,9... | collective-permute-start | bytes 2359304 | tf_op jit(solution)/shard_map/ppermute | solution.py:167
  352.6 84.1 %collective-permute-start.2 = (f32[32,3,2,1024]{3,0,2,1:T(8,128)}, f32[32,3,2,1024]{3,0,2,1:T(8,128)}, u32[]{:S(2)}, u32[]{:S(2)}) collective-permute-start(f32[32,3,2,1024]{3,0,2,1:T(8,128)} %collective-permute-done), channel_id=1, source_target_pairs={{0,1},{1,2},{2,3},{3,0},{4,5},{5,6},{6,7},{7,4},{8,9},{9,10},{10,1... | collective-permute-start | bytes 2359304 | tf_op jit(solution)/shard_map/ppermute | solution.py:162
  465.4 5.7 copy-start
  471.2 262.9 %all-reduce.25.cloned.1.call-start = ((), (), s32[]{:S(2)}) async-start(), calls=%async_computation.9 | async-start | bytes 786432 | tf_op jit(solution)/shard_map/psum | solution.py:194
  565.6 14.5 %slice-start = ((s8[6291456]{0:T(1024)(128)(4,1)}), s8[4194304]{0:T(1024)(128)(4,1)S(1)}, s32[]{:S(2)}) async-start(s8[6291456]{0:T(1024)(128)(4,1)} %bitcast.108), calls=%async_computation.10 | async-start | bytes 8388608
  570.5 6.4 copy-start.15
  570.5 9.6 %slice-start.1 = ((s8[6291456]{0:T(1024)(128)(4,1)}), s8[2097152]{0:T(1024)(128)(4,1)S(1)}, s32[]{:S(2)}) async-start(s8[6291456]{0:T(1024)(128)(4,1)} %bitcast.108), calls=%async_computation.11 | async-start | bytes 4194304
  570.7 69.0 %collective-permute-start.3 = (f32[128,3,1,1024]{3,0,2,1:T(8,128)S(1)}, f32[128,3,1,1024]{3,0,2,1:T(8,128)S(1)}, u32[]{:S(2)}, u32[]{:S(2)}) collective-permute-start(f32[128,3,1,1024]{3,0,2,1:T(8,128)S(1)} %get-tuple-element.21), channel_id=1, source_target_pairs={{0,4},{4,8},{8,12},{12,16},{16,20},{20,24},{24,28},{1,5},{5,9},{9,... | collective-permute-start | bytes 4718600 | tf_op jit(solution)/shard_map/ppermute | solution.py:17
  574.3 65.4 %collective-permute-start.4 = (f32[128,3,1,1024]{3,0,2,1:T(8,128)S(1)}, f32[128,3,1,1024]{3,0,2,1:T(8,128)S(1)}, u32[]{:S(2)}, u32[]{:S(2)}) collective-permute-start(f32[128,3,1,1024]{3,0,2,1:T(8,128)S(1)} %get-tuple-element.22), channel_id=1, source_target_pairs={{4,0},{8,4},{12,8},{16,12},{20,16},{24,20},{28,24},{5,1},{9,5},{13... | collective-permute-start | bytes 4718600 | tf_op jit(solution)/shard_map/ppermute | solution.py:18
  576.9 10.3 %copy-start.1 = (f32[32,3,2,1024]{3,0,2,1:T(8,128)}, f32[32,3,2,1024]{3,0,2,1:T(8,128)S(1)}, u32[]{:S(2)}) copy-start(f32[32,3,2,1024]{3,0,2,1:T(8,128)S(1)} %constant_dynamic-slice_fusion) | copy-start | bytes 2359300
  653.4 7.3 copy-start.9
  661.5 6.0 copy-start.5
  661.5 6.0 copy-start.7
  661.5 6.0 copy-start.10
  (9 other events, 35.5 us)
Sparse Core Ops, SparseCore 0:
  10.1 31.2 all-gather.2
  52.3 69.6 all-reduce.18
  133.4 37.2 reduce-scatter.2
  173.1 28.5 all-gather.4
  212.5 69.6 all-reduce.20
  293.6 37.2 reduce-scatter.4
  471.3 69.3 all-reduce.22
  661.6 72.4 all-reduce.24
